TPU v7x, 128 devices: a whole 4x4x4 slice. The times are simulated.
128 devices in a mesh: row: 16 (over y_lo, z, core), col: 8 (over x, y_hi).
Axes of the slice: x: 4, y: 4 (y_hi: 2, y_lo: 2; y = y_hi * 2 + y_lo), z: 4, core: 2. Of those that a mesh axis runs over, the one named last changes fastest.
Arguments:
- iterate: float32 [3072, 8192], P(('row', 'col')), may hold values from -0.030835584 to 0.030835584
Outputs:
- update: float32 [3072, 8192], P(('row', 'col'))
All inputs are finite; a program needn't handle non-finite values.
Results may differ from a plain program's by a relative error of at most 0.0003.
Values sent between devices are 32-bit elements; how exact they have to be, the bound alone decides.
A program may use at most 64 MiB of HBM per device.

v0:
```python
import math

import jax
import jax.numpy as jnp
from jax import lax
from jax.sharding import PartitionSpec as P


def per_device(iterate):
    highest = lax.Precision.HIGHEST
    grid_block = lax.all_to_all(iterate, "col", split_axis=1, concat_axis=0, tiled=True)
    band_rows = grid_block.shape[0]
    rows_whole = band_rows * lax.axis_size("row")
    cols_whole = grid_block.shape[1] * lax.axis_size("col")
    partial_term = lax.dot_general(
        grid_block,
        lax.all_gather(grid_block, "row", axis=0, tiled=True),
        (((1,), (1,)), ((), ())),
        precision=highest,
        preferred_element_type=jnp.float32,
    )
    gram_band = lax.psum(partial_term, "col")

    def apply_band(matrix_band, source):
        return jnp.dot(
            matrix_band,
            lax.all_gather(source, "row", axis=0, tiled=True),
            precision=highest,
            preferred_element_type=jnp.float32,
        )

    factor = 0.2 * math.sqrt(max(rows_whole, cols_whole))
    once_applied = apply_band(gram_band, grid_block)
    twice_applied = apply_band(gram_band, once_applied)
    polished = factor * (3.4445 * grid_block - 4.775 * once_applied + 2.0315 * twice_applied)
    return lax.all_to_all(polished, "col", split_axis=0, concat_axis=1, tiled=True)


def solution(mesh):
    return jax.shard_map(
        per_device,
        mesh=mesh,
        in_specs=(P(("row", "col"), None),),
        out_specs=P(("row", "col"), None),
        check_vma=False,
    )
```

profile of v0, /device:TPU:0, one launch (start us, length us, event | category | flops | bytes accessed | tf_op | source)
XLA Modules:
  0.0 363.5 jit_solution(16196220602282747588)
XLA Ops:
  6.5 0.0 all-gather.3.cloned.1.call-start
  6.5 1.2 copy.7
  7.7 21.0 %all_to_all.38 = f32[24,8,1024]{2,0,1:T(8,128)} all-to-all(f32[24,8,1024]{2,0,1:T(8,128)S(1)} %bitcast.22), channel_id=1, replica_groups=mesh['row'=16,'col'=8] {'col'}, dimensions={1} | all-to-all | bytes 1572864 | tf_op jit(solution)/shard_map/all_to_all | solution.py:11
  28.7 0.0 all-gather.3.cloned.1.call-update
  28.7 0.0 all-reduce.2.cloned.1.call-start
  28.8 70.6 %all-gather.3.cloned.1.call-done = f32[3072,1024]{1,0:T(8,128)} async-done(((f32[192,1024]{1,0:T(8,128)}), f32[3072,1024]{1,0:T(8,128)}) %all-gather.3.cloned.1.call-update) | async-done | bytes 12582928 | tf_op jit(solution)/shard_map/all_gather | solution.py:17
  99.4 16.9 %fusion.2 = f32[192,3072]{1,0:T(8,128)} fusion(f32[192,1024]{1,0:T(8,128)} %bitcast.18, f32[3072,1024]{1,0:T(8,128)} %all-gather.3.cloned.1.call-done), kind=kOutput, calls=%fused_computation.4 | convolution fusion | flops 7247757312 | bytes 15728640 | tf_op jit(solution)/shard_map/dot_general | solution.py:15
  116.2 0.0 copy-start
  116.2 0.0 all-reduce.2.cloned.1.call-update
  116.3 0.2 all-gather.5.cloned.1.call-start
  116.5 119.4 %all-reduce.2.cloned.1.call-done = f32[192,3072]{1,0:T(8,128)} async-done(((f32[192,3072]{1,0:T(8,128)}), f32[192,3072]{1,0:T(8,128)}) %all-reduce.2.cloned.1.call-update) | async-done | bytes 2359312 | tf_op jit(solution)/shard_map/psum | solution.py:22
  235.9 0.0 copy-start.1
  235.9 14.5 %fusion.3 = f32[192,1024]{1,0:T(8,128)} fusion(f32[192,3072]{1,0:T(8,128)} %all-reduce.2.cloned.1.call-done, f32[3072,1024]{1,0:T(8,128)} %all-gather.3.cloned.1.call-done), kind=kOutput, calls=%fused_computation.5 | convolution fusion | flops 7247757312 | bytes 15728640 | tf_op jit(solution)/shard_map/dot_general | solution.py:25
  250.5 0.0 all-gather.5.cloned.1.call-update
  250.5 72.6 %all-gather.5.cloned.1.call-done = f32[3072,1024]{1,0:T(8,128)} async-done(((f32[192,1024]{1,0:T(8,128)}), f32[3072,1024]{1,0:T(8,128)}) %all-gather.5.cloned.1.call-update) | async-done | bytes 12582928 | tf_op jit(solution)/shard_map/all_gather | solution.py:27
  323.1 0.0 copy-done
  323.1 0.0 copy-done.1
  323.1 11.9 %fusion.1 = f32[192,1024]{1,0:T(8,128)S(1)} fusion(f32[192,3072]{1,0:T(8,128)S(1)} %copy-done.1, f32[3072,1024]{1,0:T(8,128)} %all-gather.5.cloned.1.call-done, f32[192,1024]{1,0:T(8,128)} %fusion.3, f32[192,1024]{1,0:T(8,128)S(1)} %bitcast.19), kind=kOutput, calls=%fused_computation.2 | convolution fusion | flops 7248936960 | bytes 17301504 | tf_op jit(solution)/shard_map/dot_general | solution.py:25
  335.1 21.0 %all_to_all.39 = f32[8,24,1024]{2,1,0:T(8,128)S(1)} all-to-all(f32[8,24,1024]{2,1,0:T(8,128)S(1)} %bitcast.20), channel_id=1, replica_groups=mesh['row'=16,'col'=8] {'col'}, dimensions={0} | all-to-all | bytes 1572864 | tf_op jit(solution)/shard_map/all_to_all | solution.py:36
  356.1 0.9 copy.5
Async XLA Ops:
  6.5 92.8 %all-gather.3.cloned.1.call-start = ((), (), s32[]{:S(2)}) async-start(), calls=%async_computation.2 | async-start | bytes 13369344 | tf_op jit(solution)/shard_map/all_gather | solution.py:17
  28.7 207.2 %all-reduce.2.cloned.1.call-start = ((), (), s32[]{:S(2)}) async-start(), calls=%async_computation.3 | async-start | bytes 4718592 | tf_op jit(solution)/shard_map/psum | solution.py:22
  116.2 206.9 %copy-start = (f32[24,8,1024]{2,0,1:T(8,128)S(1)}, f32[24,8,1024]{2,0,1:T(8,128)}, u32[]{:S(2)}) copy-start(f32[24,8,1024]{2,0,1:T(8,128)} %all_to_all.38) | copy-start | bytes 2359300
  116.3 206.9 %all-gather.5.cloned.1.call-start = ((), (), s32[]{:S(2)}) async-start(), calls=%async_computation.4 | async-start | bytes 13369344 | tf_op jit(solution)/shard_map/all_gather | solution.py:27
  235.9 87.2 %copy-start.1 = (f32[192,3072]{1,0:T(8,128)S(1)}, f32[192,3072]{1,0:T(8,128)}, u32[]{:S(2)}) copy-start(f32[192,3072]{1,0:T(8,128)} %all-reduce.2.cloned.1.call-done) | copy-start | bytes 7077892
Sparse Core Ops, SparseCore 0:
  28.8 70.4 all-gather.2
  116.4 119.4 all-reduce.1
  250.6 72.4 all-gather.4
where the time goes:
time: 364 us
  waiting for transfers between devices  263 us (72%)
  matrix products  43.4 us (12%)
  blocking collectives  41.9 us (12%)
  between operations  13.1 us (4%)
    psum x1, waiting for transfers between devices, per_device(): gram_band = lax.psum(partial_term, 'col')  119 us
    all_gather x1, waiting for transfers between devices, apply_band(): lax.all_gather(source, 'row', axis=0, tiled=True)  72.6 us
    all_gather x1, waiting for transfers between devices, per_device(): lax.all_gather(grid_block, 'row', axis=0, tiled=True)  70.6 us
    dot_general x2, matrix products, apply_band(): jnp.dot(matrix_band, lax.all_gather(source, 'row', axis=0, tiled=True), p...  26.5 us
    all_to_all x1, blocking collectives, per_device(): lax.all_to_all(polished, 'col', split_axis=0, concat_axis=1, tiled=True)  21 us
    all_to_all x1, blocking collectives, per_device(): lax.all_to_all(iterate, 'col', split_axis=1, concat_axis=0, tiled=True)  21 us
    dot_general x1, matrix products, per_device(): lax.dot_general(grid_block, lax.all_gather(grid_block, 'row', axis=0, til...  16.9 us
  transfers between devices with their start and end apart: 3, of which 3 were waited for; matrix products, arithmetic and copies ran while one was open for 0% of the time, Pallas kernels for 0%

commit v1 on v0

v1 whole, which is shorter than its diff:
```python
import functools
import math

import jax
import jax.numpy as jnp
from jax import lax
from jax.experimental import pallas as pl
from jax.experimental.pallas import tpu as pltpu
from jax.sharding import Mesh, PartitionSpec as P

AXES = ("y_lo", "z", "core", "x", "y_hi")
SIDE = 4
BANDS = 8
PIECE = 24
BAND = SIDE * SIDE * PIECE
ROWS = BANDS * BAND
WIDTH = 512
COLS = SIDE * SIDE * WIDTH
FACTOR = 0.2 * math.sqrt(max(ROWS, COLS))
F32, BF16 = jnp.float32, jnp.bfloat16
MESH = pl.DeviceIdType.MESH
N_SEMS = 200


def halves(value):
    high = value.astype(BF16)
    return high, (value - high.astype(F32)).astype(BF16)


def kernel(x_ref, o_ref, X, Xh, Xl, Gp, R1, R2, S1, R3, G, Gh, Gl, O, Oh, Ol, T, ss, rs):
    x, z, core = lax.axis_index("x"), lax.axis_index("z"), lax.axis_index("core")
    y = lax.axis_index("y_hi") * 2 + lax.axis_index("y_lo")
    v = jnp.where(core == 0, y, x)
    u = jnp.where(core == 0, x, y)

    def wrap(i):
        return lax.rem(i + 4, 4)

    def place(dv=0, du=0):
        vv, uu = wrap(v + dv), wrap(u + du)
        return jnp.where(core == 0, uu, vv), jnp.where(core == 0, vv, uu)

    def device(dv=0, du=0, dz=0, other=False):
        px, py = place(dv, du)
        return {
            "x": px,
            "y_hi": py // 2,
            "y_lo": lax.rem(py, 2),
            "z": wrap(z + dz),
            "core": 1 - core if other else core,
        }

    def columns(px, py):
        return pl.ds(pl.multiple_of((px * 4 + py) * WIDTH, WIDTH), WIDTH)

    count = [0]
    started = []

    def send(src, dst, **to):
        i = count[0]
        count[0] += 1
        copy = pltpu.make_async_remote_copy(
            src_ref=src, dst_ref=dst, send_sem=ss.at[i], recv_sem=rs.at[i], device_id=device(**to), device_id_type=MESH
        )
        copy.start()
        started.append(copy)
        return copy

    plane = [(dv, du) for dv in (0, 1, 3, 2) for du in range(4) if dv or du]
    peers = [dict(dv=dv, du=du) for dv, du in plane] + [dict(dz=1), dict(dz=-1), dict(other=True)]
    barrier = pltpu.get_barrier_semaphore()
    for peer in peers:
        pl.semaphore_signal(barrier, inc=1, device_id=device(**peer), device_id_type=MESH)
    pl.semaphore_wait(barrier, len(peers))

    def band(dz=0, other=False):
        return wrap(z + dz) * 2 + (1 - core if other else core)

    mine = band()
    steps = [
        ((v, 0), (v, 1)),
        ((wrap(v - 1), 0), (wrap(v + 1), 1)),
        ((wrap(v - 1), 1), (wrap(v + 1), 0)),
        ((wrap(v + 2), 0), (wrap(v + 2), 1)),
    ]

    class Gather:
        def __init__(self, buf):
            self.buf = buf
            self.up, self.down, self.up2, self.down2 = [], [], [], []
            self.side = {}

        def part(self, b, k, i):
            vv, s = steps[k][i]
            return self.buf.at[b, vv, pl.ds(2 * s, 2)]

        def own(self, k):
            self.up.append([send(self.part(mine, k, i), self.part(mine, k, i), dz=1) for i in (0, 1)])
            down = [send(self.part(mine, k, i), self.part(mine, k, i), dz=-1) for i in (1, 0)]
            self.down.append(down[::-1])

        def relay(self, k):
            below, above = band(-1), band(1)
            self.up[k][0].wait_recv()
            self.up2.append(send(self.part(below, k, 0), self.part(below, k, 0), dz=1))
            self.down[k][1].wait_recv()
            self.down2.append(send(self.part(above, k, 1), self.part(above, k, 1), dz=-1))
            self.up[k][1].wait_recv()
            self.down[k][0].wait_recv()

        def far(self):
            for copy in self.up2 + self.down2:
                copy.wait_recv()

        def across(self, dz):
            b = band(dz)
            self.side[dz] = send(self.buf.at[b], self.buf.at[b], other=True)

    incoming = {}
    for dv, du in plane:
        incoming[dv, du] = send(x_ref.at[:, columns(*place(dv, du))], X.at[mine, v, u], dv=dv, du=du)
    X[mine, v, u] = x_ref[:, columns(x, y)]

    gx = Gather(X)
    for k, groups in enumerate(((0,), (1, 3), (), (2,))):
        for dv in groups:
            for du in range(4):
                if dv or du:
                    incoming[dv, du].wait_recv()
        gx.own(k)
    gx.across(0)

    def rows_of(b):
        return pl.multiple_of(b * BAND, BAND)

    def split(buf, high, low, b):
        def body(i, carry):
            h, l = halves(buf[b, i].reshape(SIDE * PIECE, WIDTH))
            at = pl.ds(pl.multiple_of(b * BAND + i * 96, 96), 96)
            high[at, :] = h
            low[at, :] = l
            return carry

        lax.fori_loop(0, SIDE, body, 0)

    def dot_t(a, b):
        return lax.dot_general(a, b, (((1,), (1,)), ((), ())), preferred_element_type=F32)

    def dot(a, b):
        return jnp.dot(a, b, preferred_element_type=F32)

    def gram(i, b):
        own, at = pl.ds(rows_of(mine), BAND), pl.ds(rows_of(b), BAND)
        ah, al, bh, bl = Xh[own, :], Xl[own, :], Xh[at, :], Xl[at, :]
        Gp[i] = (dot_t(ah, bh) + (dot_t(al, bh) + dot_t(ah, bl))).reshape(4, 4, PIECE, BAND)

    s1, s2, s3, t1 = {}, {}, {}, {}
    vp, vm, v2 = wrap(v + 1), wrap(v - 1), wrap(v + 2)

    def rs1(i):
        s1[i] = (
            send(Gp.at[i, v2, pl.ds(0, 2)], R1.at[i, 0], dv=1),
            send(Gp.at[i, v2, pl.ds(2, 2)], R1.at[i, 1], dv=-1),
        )

    def rs2(i):
        s1[i][0].wait_recv()
        Gp[i, vp, 0:2] += R1[i, 0]
        up = send(Gp.at[i, vp], R2.at[i, 0], dv=1)
        s1[i][1].wait_recv()
        Gp[i, vm, 2:4] += R1[i, 1]
        s2[i] = (up, send(Gp.at[i, vm], R2.at[i, 1], dv=-1))

    def rs3(i):
        for copy in s2[i]:
            copy.wait_recv()
        S1[i] = Gp[i, v] + (R2[i, 0] + R2[i, 1])
        s3[i] = [send(S1.at[i, wrap(u + d)], R3.at[i, d - 1], du=d) for d in (1, 3, 2)]

    def rs4(i, b):
        for copy in s3[i]:
            copy.wait_recv()
        G[v, b, u] = (S1[i, u] + R3[i, 0]) + (R3[i, 1] + R3[i, 2])
        t1[i] = [send(G.at[v, b, u], G.at[v, b, u], du=d) for d in (1, 3, 2)]

    order = [band(), band(0, True), band(-1), band(1), band(-1, True), band(1, True), band(2), band(2, True)]

    split(X, Xh, Xl, order[0])
    gram(0, order[0])
    rs1(0)
    gx.side[0].wait_recv()
    split(X, Xh, Xl, order[1])
    gram(1, order[1])
    rs1(1)
    rs2(0)
    rs2(1)
    gx.relay(0)
    rs3(0)
    rs3(1)
    gx.relay(1)
    rs4(0, order[0])
    rs4(1, order[1])
    gx.relay(2)
    gx.relay(3)
    gx.across(-1)
    gx.across(1)
    for i in (2, 3):
        split(X, Xh, Xl, order[i])
        gram(i, order[i])
        rs1(i)
    for i, dz in ((4, -1), (5, 1)):
        gx.side[dz].wait_recv()
        split(X, Xh, Xl, order[i])
        gram(i, order[i])
        rs1(i)
        rs2(i - 2)
    rs3(2)
    rs2(4)
    rs3(3)
    rs2(5)
    gx.far()
    gx.across(2)
    split(X, Xh, Xl, order[6])
    gram(6, order[6])
    rs1(6)
    gx.side[2].wait_recv()
    split(X, Xh, Xl, order[7])
    gram(7, order[7])
    rs1(7)
    rs3(4)
    rs3(5)
    rs2(6)
    rs2(7)
    for i in (2, 3, 4, 5):
        rs4(i, order[i])
    rs3(6)
    rs3(7)
    rs4(6, order[6])
    rs4(7, order[7])

    for i in range(BANDS):
        for copy in t1[i]:
            copy.wait_recv()

    def gram_part(part):
        return G.at[part[0], :, pl.ds(2 * part[1], 2)]

    def forward(part, dv):
        return send(gram_part(part), gram_part(part), dv=dv)

    up = [forward((v, 0), 1), forward((v, 1), 1)]
    down = [forward((v, 1), -1), forward((v, 0), -1)]

    go = Gather(O)

    def once(k):
        at = []
        for vv, s in steps[k]:
            rows = pl.ds(pl.multiple_of(vv * 96 + s * 48, 16), 48)
            at.append(rows)
            for b in range(BANDS):
                h, l = halves(G[vv, b, pl.ds(2 * s, 2)].reshape(48, BAND))
                Gh[rows, b * BAND : (b + 1) * BAND] = h
                Gl[rows, b * BAND : (b + 1) * BAND] = l
        high = [Gh[rows, :] for rows in at]
        low = [Gl[rows, :] for rows in at]
        first = dot(jnp.concatenate(high + low, axis=0), Xh[...])
        result = first[:96] + (first[96:] + dot(jnp.concatenate(high, axis=0), Xl[...]))
        for i, (vv, s) in enumerate(steps[k]):
            O[mine, vv, pl.ds(2 * s, 2)] = result[48 * i : 48 * (i + 1)].reshape(2, PIECE, WIDTH)
        go.own(k)

    once(0)
    up[0].wait_recv()
    up2 = forward((vm, 0), 1)
    down[0].wait_recv()
    down2 = forward((vp, 1), -1)
    once(1)
    go.relay(0)
    up[1].wait_recv()
    down[1].wait_recv()
    once(2)
    go.relay(1)
    up2.wait_recv()
    down2.wait_recv()
    once(3)
    go.across(0)
    go.relay(2)

    def twice(b, first=False):
        split(O, Oh, Ol, b)
        cols, at = pl.ds(pl.multiple_of(b * BAND, 128), BAND), pl.ds(rows_of(b), BAND)
        gh, gl, oh, ol = Gh[:, cols], Gl[:, cols], Oh[at, :], Ol[at, :]
        term = (dot(gh, oh) + (dot(gl, oh) + dot(gh, ol))).reshape(4, 4, PIECE, WIDTH)
        T[...] = term if first else T[...] + term

    twice(order[0], True)
    go.side[0].wait_recv()
    twice(order[1])
    go.relay(3)
    go.across(-1)
    go.across(1)
    twice(order[2])
    twice(order[3])
    go.far()
    go.across(2)
    for i, dz in ((4, -1), (5, 1)):
        go.side[dz].wait_recv()
        twice(order[i])
    twice(order[6])
    go.side[2].wait_recv()
    twice(order[7])
    T[...] = FACTOR * (3.4445 * X[mine] - 4.775 * O[mine] + 2.0315 * T[...])

    outgoing = []
    for dv, du in plane:
        outgoing.append(
            send(T.at[wrap(v + dv), wrap(u + du)], o_ref.at[:, columns(x, y)], dv=dv, du=du)
        )
    o_ref[:, columns(x, y)] = T[v, u]
    for copy in outgoing:
        copy.wait_recv()
    for copy in started:
        copy.wait_send()


def per_device(iterate):
    vmem = functools.partial(pl.BlockSpec, memory_space=pltpu.VMEM)
    shapes = [
        ((BANDS, 4, 4, PIECE, WIDTH), F32),
        ((ROWS, WIDTH), BF16),
        ((ROWS, WIDTH), BF16),
        ((BANDS, 4, 4, PIECE, BAND), F32),
        ((BANDS, 2, 2, PIECE, BAND), F32),
        ((BANDS, 2, 4, PIECE, BAND), F32),
        ((BANDS, 4, PIECE, BAND), F32),
        ((BANDS, 3, PIECE, BAND), F32),
        ((4, BANDS, 4, PIECE, BAND), F32),
        ((BAND, ROWS), BF16),
        ((BAND, ROWS), BF16),
        ((BANDS, 4, 4, PIECE, WIDTH), F32),
        ((ROWS, WIDTH), BF16),
        ((ROWS, WIDTH), BF16),
        ((4, 4, PIECE, WIDTH), F32),
    ]
    return pl.pallas_call(
        kernel,
        out_shape=jax.ShapeDtypeStruct((PIECE, COLS), F32),
        in_specs=[vmem()],
        out_specs=vmem(),
        scratch_shapes=[pltpu.VMEM(shape, dtype) for shape, dtype in shapes]
        + [pltpu.SemaphoreType.DMA((N_SEMS,)), pltpu.SemaphoreType.DMA((N_SEMS,))],
        compiler_params=pltpu.CompilerParams(
            collective_id=0, has_side_effects=True, vmem_limit_bytes=60 * 1024 * 1024
        ),
        cost_estimate=pl.CostEstimate(
            flops=6 * 3 * BAND * ROWS * WIDTH, bytes_accessed=2 * 4 * PIECE * COLS, transcendentals=0
        ),
    )(iterate)


def solution(mesh):
    fine = Mesh(mesh.devices.reshape(2, 4, 2, 4, 2), AXES)
    spec = P(AXES, None)
    return jax.shard_map(per_device, mesh=fine, in_specs=(spec,), out_specs=spec, check_vma=False)
```

time: 364 us -> 132 us (0.36)
  waiting for transfers between devices: 263 us -> 0 us
  Pallas kernels: 0 us -> 130 us
  matrix products: 43.4 us -> 0 us
  blocking collectives: 41.9 us -> 0 us
  between operations: 13.1 us -> 0.01 us
    all_gather x2 -> x0, waiting for transfers between devices: 143 us -> none  [the longest x1 72.6 us: apply_band(): lax.all_gather(source, 'row', axis=0, tiled=True)]
    pallas_call x0 -> x1, Pallas kernels: none -> 130 us  [per_device(): pl.pallas_call(kernel, out_shape=jax.ShapeDtypeStruct((PIECE, COLS), F32)...]
    psum x1 -> x0, waiting for transfers between devices: 119 us -> none  [per_device(): gram_band = lax.psum(partial_term, 'col')]
    dot_general x3 -> x0, matrix products: 43.4 us -> none  [the longest x2 26.5 us: apply_band(): jnp.dot(matrix_band, lax.all_gather(source, 'row', axis=0, tiled=True), p...]
    all_to_all x2 -> x0, blocking collectives: 41.9 us -> none  [the longest x1 21 us: per_device(): lax.all_to_all(polished, 'col', split_axis=0, concat_axis=1, tiled=True)]
  transfers between devices with their start and end apart: 3 -> 0, of which waited for: 3 -> 0; matrix products, arithmetic and copies ran while one was open for 0% -> 0% of each run, Pallas kernels for 0% -> 0%
where the time goes in v1:
time: 132 us
  Pallas kernels  130 us (98%)
  local copies, waits for them, and re-layouts  2.06 us (2%)
    pallas_call x1, Pallas kernels, per_device(): pl.pallas_call(kernel, out_shape=jax.ShapeDtypeStruct((PIECE, COLS), F32)...  130 us

profile of v1, /device:TPU:0, one launch (start us, length us, event | category | flops | bytes accessed | tf_op | source)
XLA Modules:
  0.0 132.0 jit_solution(13107619643817332678)
XLA Ops:
  0.0 130.0 %shard_map.17 = f32[24,8192]{1,0:T(8,128)} custom-call(f32[24,8192]{1,0:T(8,128)} %x_ref.1), custom_call_target="tpu_custom_call" | custom-call | flops 10871635968 | bytes 1572864 | tf_op jit(solution)/shard_map/pallas_call | solution.py:346
  130.0 2.1 %copy.3 = f32[24,8192]{1,0:T(8,128)} copy(f32[24,8192]{1,0:T(8,128)} %shard_map.17) | data formatting | bytes 1572864

commit v2 on v0

v2 whole, which is shorter than its diff:
```python
import math

import jax
import jax.numpy as jnp
from jax import lax
from jax.experimental import pallas as pl
from jax.experimental.pallas import tpu as pltpu
from jax.sharding import Mesh, PartitionSpec as P

AXES = ("y_lo", "z", "core", "x", "y_hi")
BANDS = 8
GROUPS = 3
LANES = 128
BAND = GROUPS * LANES
ROWS = BANDS * BAND
WIDTH = 512
COLS = 16 * WIDTH
FACTOR = 0.2 * math.sqrt(max(ROWS, COLS))
F32, BF16 = jnp.float32, jnp.bfloat16
MESH = pl.DeviceIdType.MESH
N_SEMS = 136
UNITS = (3, 3, 4, 4, 4, 2, 2, 2)
FIRST = tuple(sum(UNITS[:c]) for c in range(len(UNITS)))
CHUNK = tuple(slice(LANES * a, LANES * (a + n)) for a, n in zip(FIRST, UNITS))
ORDER = (
    "z0 z1 z2 g0",
    "g1 r0 a0 p0",
    "g2 p1 r1 a1",
    "s0 p2 g3 s1",
    "q0 r2 a2 s2",
    "p3 g4 f0 q1",
    "g5 q2 f1 s3",
    "g6 p4 f2 p5",
    "g7 p6 q3 s4",
    "s5 p7 s6 q4",
    "q5 s7 q6 q7",
)


def halves(value):
    high = value.astype(BF16)
    return high, (value - high.astype(F32)).astype(BF16)


def kernel(x_ref, o_ref, X, Xh, Xl, Gp, R1, R2, S1, R3, G, Gh, Gl, O, Oh, Ol, T, ss, rs):
    x, z, core = lax.axis_index("x"), lax.axis_index("z"), lax.axis_index("core")
    y = lax.axis_index("y_hi") * 2 + lax.axis_index("y_lo")
    v = jnp.where(core == 0, y, x)
    u = jnp.where(core == 0, x, y)

    def wrap(i):
        return lax.rem(i + 4, 4)

    def place(dv=0, du=0):
        vv, uu = wrap(v + dv), wrap(u + du)
        return jnp.where(core == 0, uu, vv), jnp.where(core == 0, vv, uu)

    def device(dv=0, du=0, dz=0, other=False):
        px, py = place(dv, du)
        return {
            "x": px,
            "y_hi": py // 2,
            "y_lo": lax.rem(py, 2),
            "z": wrap(z + dz),
            "core": 1 - core if other else core,
        }

    def columns(px, py):
        return pl.ds(pl.multiple_of((px * 4 + py) * WIDTH, WIDTH), WIDTH)

    count = [0]
    leaving = []

    def fresh(size):
        i = count[0]
        count[0] += 1
        leaving.append((i, size))
        return i

    def send(i, src, dst, **to):
        pltpu.make_async_remote_copy(
            src_ref=src, dst_ref=dst, send_sem=ss.at[i], recv_sem=rs.at[i], device_id=device(**to), device_id_type=MESH
        ).start()

    def send_one(src, dst, **to):
        i = fresh(src)
        send(i, src, dst, **to)
        return i, src

    def arrive(pair):
        i, size = pair
        pltpu.make_async_copy(size, size, rs.at[i]).wait()

    plane = [(dv, du) for dv in (0, 1, 3, 2) for du in range(4) if dv or du]
    peers = [dict(dv=dv, du=du) for dv, du in plane] + [dict(dz=1), dict(dz=-1), dict(other=True)]
    barrier = pltpu.get_barrier_semaphore()
    for peer in peers:
        pl.semaphore_signal(barrier, inc=1, device_id=device(**peer), device_id_type=MESH)
    pl.semaphore_wait(barrier, len(peers))

    def band(dz=0, other=False):
        return wrap(z + dz) * 2 + (1 - core if other else core)

    mine, sibling = band(), band(0, True)
    near = [band(-1), band(1), band(-1, True), band(1, True)]
    away = [band(2), band(2, True)]
    rows = [[(mine, j) for j in range(GROUPS)], [(sibling, j) for j in range(GROUPS)]]
    rows += [[(b, j) for b in near] for j in range(GROUPS)]
    rows += [[(b, j) for b in away] for j in range(GROUPS)]

    i_out = fresh(x_ref.at[:, :, pl.ds(0, 15 * WIDTH)])
    i_in = [i_out, count[0], count[0] + 1]
    count[0] += 2
    for j in range(GROUPS):
        for dv, du in plane:
            pltpu.make_async_remote_copy(
                src_ref=x_ref.at[j, :, columns(*place(dv, du))],
                dst_ref=X.at[mine, j, v, u],
                send_sem=ss.at[i_out],
                recv_sem=rs.at[i_in[j]],
                device_id=device(dv=dv, du=du),
                device_id_type=MESH,
            ).start()
        pltpu.make_async_copy(x_ref.at[j, :, columns(x, y)], X.at[mine, j, v, u], rs.at[i_in[j]]).start()

    def dot_t(a, b):
        return lax.dot_general(a, b, (((1,), (1,)), ((), ())), preferred_element_type=F32)

    def dot(a, b):
        return jnp.dot(a, b, preferred_element_type=F32)

    def split(buf, high, low, c):
        for i, (b, j) in enumerate(rows[c]):
            at = slice((FIRST[c] + i) * LANES, (FIRST[c] + i + 1) * LANES)
            high[at, :], low[at, :] = halves(buf[b, j].reshape(LANES, WIDTH))

    vp, vm, v2 = wrap(v + 1), wrap(v - 1), wrap(v + 2)
    up, down, up2, down2, side = {}, {}, {}, {}, {}
    r1, r2, r3, r4 = {}, {}, {}, {}
    side["own"] = (fresh(X.at[0]), X.at[0])

    def z_step(j):
        part = X.at[mine, j]
        arrive((i_in[j], part))
        up[j] = send_one(part, part, dz=1)
        down[j] = send_one(part, part, dz=-1)
        send(side["own"][0], part, part, other=True)

    def r_step(j):
        arrive(up[j])
        half = X.at[near[0], j, pl.ds(0, 2)]
        up2[j] = send_one(half, half, dz=1)
        arrive(down[j])
        half = X.at[near[1], j, pl.ds(2, 2)]
        down2[j] = send_one(half, half, dz=-1)

    def a_step(j):
        side[j] = (fresh(X.at[0, pl.ds(0, 2)]), X.at[0, pl.ds(0, 2)])
        for b in near[:2]:
            send(side[j][0], X.at[b, j], X.at[b, j], other=True)

    def f_step(j):
        arrive(up2[j])
        arrive(down2[j])
        part = X.at[away[0], j]
        side[GROUPS + j] = send_one(part, part, other=True)

    def g_step(c):
        if c:
            arrive(side["own" if c == 1 else c - 2])
        split(X, Xh, Xl, c)
        at = CHUNK[c]
        ah, al, bh, bl = Xh[:BAND, :], Xl[:BAND, :], Xh[at, :], Xl[at, :]
        term = dot_t(ah, bh) + (dot_t(al, bh) + dot_t(ah, bl))
        Gp[:, :, :, :, at] = term.reshape(GROUPS, 4, 4, 8, LANES * UNITS[c])
        r1[c] = (
            send_one(Gp.at[:, v2, pl.ds(0, 2), :, at], R1.at[0, :, :, :, at], dv=1),
            send_one(Gp.at[:, v2, pl.ds(2, 2), :, at], R1.at[1, :, :, :, at], dv=-1),
        )

    def p_step(c):
        at = CHUNK[c]
        arrive(r1[c][0])
        Gp[:, vp, 0:2, :, at] += R1[0, :, :, :, at]
        first = send_one(Gp.at[:, vp, :, :, at], R2.at[0, :, :, :, at], dv=1)
        arrive(r1[c][1])
        Gp[:, vm, 2:4, :, at] += R1[1, :, :, :, at]
        r2[c] = (first, send_one(Gp.at[:, vm, :, :, at], R2.at[1, :, :, :, at], dv=-1))

    def s_step(c):
        at = CHUNK[c]
        for pair in r2[c]:
            arrive(pair)
        S1[:, :, :, at] = Gp[:, v, :, :, at] + (R2[0, :, :, :, at] + R2[1, :, :, :, at])
        size = R3.at[:, :, :, at]
        r3[c] = (fresh(size), size)
        for d in (1, 3, 2):
            send(r3[c][0], S1.at[:, wrap(u + d), :, at], R3.at[d - 1, :, :, at], du=d)

    def q_step(c):
        at = CHUNK[c]
        arrive(r3[c])
        G[:, v, u, :, at] = (S1[:, u, :, at] + R3[0, :, :, at]) + (R3[1, :, :, at] + R3[2, :, :, at])
        r4[c] = (fresh(r3[c][1]), r3[c][1])
        mine_of = G.at[:, v, u, :, at]
        for d in (1, 3, 2):
            send(r4[c][0], mine_of, mine_of, du=d)

    steps = dict(z=z_step, r=r_step, a=a_step, f=f_step, g=g_step, p=p_step, s=s_step, q=q_step)
    for line in ORDER:
        for step in line.split():
            steps[step[0]](int(step[1:]))
    for c in range(len(UNITS)):
        arrive(r4[c])

    def forward(vv, uu, dv):
        part = G.at[:, vv, uu]
        return send_one(part, part, dv=dv)

    rise = [forward(v, i, 1) for i in range(4)]
    fall = [forward(v, 3 - i, -1) for i in range(4)]
    rise2, fall2 = [], []

    takes = [((v, 0, 2), (v, 2, 2))]
    takes += [((vm, i, 1), (vp, 3 - i, 1)) for i in range(4)]
    takes += [((v2, i, 1), (v2, 3 - i, 1)) for i in range(2)]
    o_up, o_down, o_up2, o_down2 = [], [], [], []
    o_side = {key: (fresh(O.at[0]), O.at[0]) for key in ("own", "low", "high", "far")}

    def part_of(b, take):
        vv, first, n = take
        return O.at[b, :, vv, pl.ds(first, n)]

    def across(key, b, *parts):
        for take in parts:
            send(o_side[key][0], part_of(b, take), part_of(b, take), other=True)

    def once(k):
        at = []
        for vv, first, n in takes[k]:
            for j in range(GROUPS):
                h, l = halves(G[j, vv, pl.ds(first, n)].reshape(8 * n, ROWS))
                at.append((j, vv, first, n, h, l))
        high = jnp.concatenate([part[4] for part in at], axis=0)
        low = jnp.concatenate([part[5] for part in at], axis=0)
        m = high.shape[0]
        first_two = dot(jnp.concatenate([high, low], axis=0), Xh[...])
        result = first_two[:m] + (first_two[m:] + dot(high, Xl[...]))
        row = 0
        for j, vv, first, n, _, _ in at:
            O[mine, j, vv, pl.ds(first, n)] = result[row : row + 8 * n].reshape(n, 8, WIDTH)
            row += 8 * n
        a, b = takes[k]
        size = O.at[0, :, 0, pl.ds(0, 2 * a[2])]
        o_up.append((fresh(size), size))
        o_down.append((fresh(size), size))
        for take in (a, b):
            send(o_up[k][0], part_of(mine, take), part_of(mine, take), dz=1)
        for take in (b, a):
            send(o_down[k][0], part_of(mine, take), part_of(mine, take), dz=-1)
        across("own", mine, a, b)

    def pass_on(k):
        a, b = takes[k]
        arrive(o_up[k])
        o_up2.append(send_one(part_of(near[0], a), part_of(near[0], a), dz=1))
        arrive(o_down[k])
        o_down2.append(send_one(part_of(near[1], b), part_of(near[1], b), dz=-1))
        across("low", near[0], a, b)
        across("high", near[1], a, b)

    def far(k):
        arrive(o_up2[k])
        arrive(o_down2[k])
        across("far", away[0], *takes[k])

    once(0)
    for k in range(1, 7):
        if k < 5:
            arrive(rise[k - 1])
            if k < 3:
                rise2.append(forward(vm, k - 1, 1))
            arrive(fall[k - 1])
            if k < 3:
                fall2.append(forward(vp, 4 - k, -1))
        else:
            arrive(rise2[k - 5])
            arrive(fall2[k - 5])
        once(k)
        if k > 1:
            pass_on(k - 2)
        if k > 3:
            far(k - 4)
    for j in range(GROUPS):
        at = slice(j * LANES, (j + 1) * LANES)
        Gh[at, :], Gl[at, :] = halves(G[j].reshape(LANES, ROWS))

    def twice(c):
        split(O, Oh, Ol, c)
        at = CHUNK[c]
        gh, gl, oh, ol = Gh[:, at], Gl[:, at], Oh[at, :], Ol[at, :]
        term = (dot(gh, oh) + (dot(gl, oh) + dot(gh, ol))).reshape(GROUPS, 4, 4, 8, WIDTH)
        T[...] = T[...] + term if c else term

    twice(0)
    pass_on(5)
    far(3)
    arrive(o_side["own"])
    twice(1)
    pass_on(6)
    far(4)
    arrive(o_side["low"])
    arrive(o_side["high"])
    for c in (2, 3, 4):
        twice(c)
    far(5)
    far(6)
    arrive(o_side["far"])
    for c in (5, 6, 7):
        twice(c)
    T[...] = FACTOR * (3.4445 * X[mine] - 4.775 * O[mine] + 2.0315 * T[...])

    i_out = fresh(o_ref.at[:, :, pl.ds(0, 15 * WIDTH)])
    mine_at = o_ref.at[:, :, columns(x, y)]
    for dv, du in plane:
        send(i_out, T.at[:, wrap(v + dv), wrap(u + du)], mine_at, dv=dv, du=du)
    pltpu.make_async_copy(T.at[:, v, u], mine_at, rs.at[i_out]).start()
    arrive((i_out, o_ref))
    for i, size in leaving:
        pltpu.make_async_copy(size, size, ss.at[i]).wait()
    if count[0] > N_SEMS:
        raise ValueError(count[0])


def per_device(iterate):
    vmem = pl.BlockSpec(memory_space=pltpu.VMEM)
    whole, gram, band = (BANDS, GROUPS, 4, 4, 8, WIDTH), (GROUPS, 4, 4, 8, ROWS), (BAND, ROWS)
    shapes = [
        (whole, F32),
        ((ROWS, WIDTH), BF16),
        ((ROWS, WIDTH), BF16),
        (gram, F32),
        ((2, GROUPS, 2, 8, ROWS), F32),
        ((2, GROUPS, 4, 8, ROWS), F32),
        ((GROUPS, 4, 8, ROWS), F32),
        ((3, GROUPS, 8, ROWS), F32),
        (gram, F32),
        (band, BF16),
        (band, BF16),
        (whole, F32),
        ((ROWS, WIDTH), BF16),
        ((ROWS, WIDTH), BF16),
        ((GROUPS, 4, 4, 8, WIDTH), F32),
    ]
    update = pl.pallas_call(
        kernel,
        out_shape=jax.ShapeDtypeStruct((GROUPS, 8, COLS), F32),
        in_specs=[vmem],
        out_specs=vmem,
        scratch_shapes=[pltpu.VMEM(shape, dtype) for shape, dtype in shapes]
        + [pltpu.SemaphoreType.DMA((N_SEMS,)), pltpu.SemaphoreType.DMA((N_SEMS,))],
        compiler_params=pltpu.CompilerParams(
            collective_id=0, has_side_effects=True, vmem_limit_bytes=50 * 1024 * 1024
        ),
        cost_estimate=pl.CostEstimate(
            flops=6 * 3 * BAND * ROWS * WIDTH, bytes_accessed=2 * 4 * GROUPS * 8 * COLS, transcendentals=0
        ),
    )(iterate.reshape(GROUPS, 8, COLS))
    return update.reshape(GROUPS * 8, COLS)


def solution(mesh):
    fine = Mesh(mesh.devices.reshape(2, 4, 2, 4, 2), AXES)
    spec = P(AXES, None)
    return jax.shard_map(per_device, mesh=fine, in_specs=(spec,), out_specs=spec, check_vma=False)
```

time: 364 us -> 121 us (0.33)
  waiting for transfers between devices: 263 us -> 0 us
  Pallas kernels: 0 us -> 119 us
  matrix products: 43.4 us -> 0 us
  blocking collectives: 41.9 us -> 0 us
  between operations: 13.1 us -> 0.01 us
    all_gather x2 -> x0, waiting for transfers between devices: 143 us -> none  [the longest x1 72.6 us: apply_band(): lax.all_gather(source, 'row', axis=0, tiled=True)]
    psum x1 -> x0, waiting for transfers between devices: 119 us -> none  [per_device(): gram_band = lax.psum(partial_term, 'col')]
    pallas_call x0 -> x1, Pallas kernels: none -> 119 us  [per_device(): pl.pallas_call(kernel, out_shape=jax.ShapeDtypeStruct((GROUPS, 8, COLS),...]
    dot_general x3 -> x0, matrix products: 43.4 us -> none  [the longest x2 26.5 us: apply_band(): jnp.dot(matrix_band, lax.all_gather(source, 'row', axis=0, tiled=True), p...]
    all_to_all x2 -> x0, blocking collectives: 41.9 us -> none  [the longest x1 21 us: per_device(): lax.all_to_all(polished, 'col', split_axis=0, concat_axis=1, tiled=True)]
  transfers between devices with their start and end apart: 3 -> 0, of which waited for: 3 -> 0; matrix products, arithmetic and copies ran while one was open for 0% -> 0% of each run, Pallas kernels for 0% -> 0%
where the time goes in v2:
time: 121 us
  Pallas kernels  119 us (98%)
  local copies, waits for them, and re-layouts  2.01 us (2%)
    pallas_call x1, Pallas kernels, per_device(): pl.pallas_call(kernel, out_shape=jax.ShapeDtypeStruct((GROUPS, 8, COLS),...  119 us

profile of v2, /device:TPU:0, one launch (start us, length us, event | category | flops | bytes accessed | tf_op | source)
XLA Modules:
  0.0 120.9 jit_solution(5226796439028034510)
XLA Ops:
  0.0 0.0 copy-start
  0.0 1.1 copy-done
  1.1 118.9 %shard_map.17 = f32[3,8,8192]{2,1,0:T(8,128)S(1)} custom-call(f32[3,8,8192]{2,1,0:T(8,128)S(1)} %bitcast.3), custom_call_target="tpu_custom_call" | custom-call | flops 10871635968 | bytes 1572864 | tf_op jit(solution)/shard_map/pallas_call | solution.py:355
  120.0 0.9 copy.3
Async XLA Ops:
  0.0 1.1 copy-start

commit v3 on v2

--- a/solution.py
+++ b/solution.py
@@ -18,22 +18,25 @@
 FACTOR = 0.2 * math.sqrt(max(ROWS, COLS))
 F32, BF16 = jnp.float32, jnp.bfloat16
 MESH = pl.DeviceIdType.MESH
-N_SEMS = 136
+N_SEMS = 117
 UNITS = (3, 3, 4, 4, 4, 2, 2, 2)
 FIRST = tuple(sum(UNITS[:c]) for c in range(len(UNITS)))
 CHUNK = tuple(slice(LANES * a, LANES * (a + n)) for a, n in zip(FIRST, UNITS))
+LAST = len(UNITS) - 1
+PLANE = (2, 2), (0, 1), (1, 0), (2, 1), (3, 2), (1, 2), (2, 3), (0, 3), (3, 0), (1, 1), (3, 3), (0, 2), (2, 0), (1, 3), (3, 1)
 ORDER = (
-    "z0 z1 z2 g0",
-    "g1 r0 a0 p0",
-    "g2 p1 r1 a1",
-    "s0 p2 g3 s1",
-    "q0 r2 a2 s2",
-    "p3 g4 f0 q1",
-    "g5 q2 f1 s3",
-    "g6 p4 f2 p5",
-    "g7 p6 q3 s4",
-    "s5 p7 s6 q4",
-    "q5 s7 q6 q7",
+    "y0 z0 z1 z2",
+    "g0 g1 r0 a0",
+    "p0 g2 p1 r1",
+    "a1 s0 g3 p2",
+    "s1 r2 a2 q0",
+    "g4 f0 p3 g5",
+    "s2 f1 q1 g6",
+    "p4 f2 s3 p5",
+    "g7 q2 p6 s4",
+    "q3 s5 p7 s6",
+    "q4 q5 s7 q6",
+    "q7",
 )
 
 
@@ -42,7 +45,7 @@
     return high, (value - high.astype(F32)).astype(BF16)
 
 
-def kernel(x_ref, o_ref, X, Xh, Xl, Gp, R1, R2, S1, R3, G, Gh, Gl, O, Oh, Ol, T, ss, rs):
+def kernel(x_ref, o_ref, X, Xh, Xl, Gp, R1, R2, S1, R3, R4, G, Gh, Gl, O, Oh, Ol, T, ss, rs):
     x, z, core = lax.axis_index("x"), lax.axis_index("z"), lax.axis_index("core")
     y = lax.axis_index("y_hi") * 2 + lax.axis_index("y_lo")
     v = jnp.where(core == 0, y, x)
@@ -91,8 +94,7 @@
         i, size = pair
         pltpu.make_async_copy(size, size, rs.at[i]).wait()
 
-    plane = [(dv, du) for dv in (0, 1, 3, 2) for du in range(4) if dv or du]
-    peers = [dict(dv=dv, du=du) for dv, du in plane] + [dict(dz=1), dict(dz=-1), dict(other=True)]
+    peers = [dict(dv=dv, du=du) for dv, du in PLANE] + [dict(dz=1), dict(dz=-1), dict(other=True)]
     barrier = pltpu.get_barrier_semaphore()
     for peer in peers:
         pl.semaphore_signal(barrier, inc=1, device_id=device(**peer), device_id_type=MESH)
@@ -109,19 +111,26 @@
     rows += [[(b, j) for b in away] for j in range(GROUPS)]
 
     i_out = fresh(x_ref.at[:, :, pl.ds(0, 15 * WIDTH)])
-    i_in = [i_out, count[0], count[0] + 1]
-    count[0] += 2
+    i_in = [i_out, count[0], count[0] + 1, count[0] + 2]
+    count[0] += 3
+
+    def scatter(i, groups, dv, du):
+        pltpu.make_async_remote_copy(
+            src_ref=x_ref.at[groups, :, columns(*place(dv, du))],
+            dst_ref=X.at[mine, groups, v, u],
+            send_sem=ss.at[i_out],
+            recv_sem=rs.at[i],
+            device_id=device(dv=dv, du=du),
+            device_id_type=MESH,
+        ).start()
+
+    for du in (1, 3, 2):
+        scatter(i_in[3], pl.ds(0, GROUPS), 0, du)
+    pltpu.make_async_copy(x_ref.at[:, :, columns(x, y)], X.at[mine, :, v, u], rs.at[i_in[3]]).start()
     for j in range(GROUPS):
-        for dv, du in plane:
-            pltpu.make_async_remote_copy(
-                src_ref=x_ref.at[j, :, columns(*place(dv, du))],
-                dst_ref=X.at[mine, j, v, u],
-                send_sem=ss.at[i_out],
-                recv_sem=rs.at[i_in[j]],
-                device_id=device(dv=dv, du=du),
-                device_id_type=MESH,
-            ).start()
-        pltpu.make_async_copy(x_ref.at[j, :, columns(x, y)], X.at[mine, j, v, u], rs.at[i_in[j]]).start()
+        for dv, du in PLANE:
+            if dv:
+                scatter(i_in[j], j, dv, du)
 
     def dot_t(a, b):
         return lax.dot_general(a, b, (((1,), (1,)), ((), ())), preferred_element_type=F32)
@@ -139,14 +148,28 @@
     r1, r2, r3, r4 = {}, {}, {}, {}
     side["own"] = (fresh(X.at[0]), X.at[0])
 
+    first = X.at[mine, :, v]
+    i_first = [fresh(first), fresh(first)]
+
+    def y_step(_):
+        arrive((i_in[3], first))
+        send(i_first[0], first, first, dz=1)
+        send(i_first[1], first, first, dz=-1)
+        send(side["own"][0], first, first, other=True)
+
     def z_step(j):
-        part = X.at[mine, j]
-        arrive((i_in[j], part))
-        up[j] = send_one(part, part, dz=1)
-        down[j] = send_one(part, part, dz=-1)
-        send(side["own"][0], part, part, other=True)
+        size = X.at[0, j, pl.ds(0, 3)]
+        arrive((i_in[j], size))
+        up[j], down[j] = (fresh(size), size), (fresh(size), size)
+        for to, i in ((dict(dz=1), up[j][0]), (dict(dz=-1), down[j][0]), (dict(other=True), side["own"][0])):
+            for vv in (vp, v2, vm):
+                part = X.at[mine, j, vv]
+                send(i, part, part, **to)
 
     def r_step(j):
+        if j == 0:
+            arrive((i_first[0], first))
+            arrive((i_first[1], first))
         arrive(up[j])
         half = X.at[near[0], j, pl.ds(0, 2)]
         up2[j] = send_one(half, half, dz=1)
@@ -192,6 +215,11 @@
         for pair in r2[c]:
             arrive(pair)
         S1[:, :, :, at] = Gp[:, v, :, :, at] + (R2[0, :, :, :, at] + R2[1, :, :, :, at])
+        if c == LAST:
+            r3[c] = (fresh(R4), R4)
+            for d in (1, 3, 2):
+                send(r3[c][0], S1.at[:, :, :, at], R4.at[d - 1], du=d)
+            return
         size = R3.at[:, :, :, at]
         r3[c] = (fresh(size), size)
         for d in (1, 3, 2):
@@ -200,17 +228,20 @@
     def q_step(c):
         at = CHUNK[c]
         arrive(r3[c])
+        if c == LAST:
+            G[:, v, :, :, at] = (S1[:, :, :, at] + R4[0]) + (R4[1] + R4[2])
+            return
         G[:, v, u, :, at] = (S1[:, u, :, at] + R3[0, :, :, at]) + (R3[1, :, :, at] + R3[2, :, :, at])
         r4[c] = (fresh(r3[c][1]), r3[c][1])
         mine_of = G.at[:, v, u, :, at]
         for d in (1, 3, 2):
             send(r4[c][0], mine_of, mine_of, du=d)
 
-    steps = dict(z=z_step, r=r_step, a=a_step, f=f_step, g=g_step, p=p_step, s=s_step, q=q_step)
+    steps = dict(y=y_step, z=z_step, r=r_step, a=a_step, f=f_step, g=g_step, p=p_step, s=s_step, q=q_step)
     for line in ORDER:
         for step in line.split():
             steps[step[0]](int(step[1:]))
-    for c in range(len(UNITS)):
+    for c in range(LAST):
         arrive(r4[c])
 
     def forward(vv, uu, dv):
@@ -320,13 +351,16 @@
         twice(c)
     T[...] = FACTOR * (3.4445 * X[mine] - 4.775 * O[mine] + 2.0315 * T[...])
 
+    before = list(leaving)
     i_out = fresh(o_ref.at[:, :, pl.ds(0, 15 * WIDTH)])
     mine_at = o_ref.at[:, :, columns(x, y)]
-    for dv, du in plane:
+    for dv, du in PLANE:
         send(i_out, T.at[:, wrap(v + dv), wrap(u + du)], mine_at, dv=dv, du=du)
     pltpu.make_async_copy(T.at[:, v, u], mine_at, rs.at[i_out]).start()
+    for i, size in before:
+        pltpu.make_async_copy(size, size, ss.at[i]).wait()
     arrive((i_out, o_ref))
-    for i, size in leaving:
+    for i, size in leaving[len(before) :]:
         pltpu.make_async_copy(size, size, ss.at[i]).wait()
     if count[0] > N_SEMS:
         raise ValueError(count[0])
@@ -344,6 +378,7 @@
         ((2, GROUPS, 4, 8, ROWS), F32),
         ((GROUPS, 4, 8, ROWS), F32),
         ((3, GROUPS, 8, ROWS), F32),
+        ((3, GROUPS, 4, 8, LANES * UNITS[-1]), F32),
         (gram, F32),
         (band, BF16),
         (band, BF16),

time: 121 us -> 117 us (0.967); the launches traced: 121 us -> 115 us
  Pallas kernels: 119 us -> 113 us
    pallas_call x1, Pallas kernels: 119 us -> 113 us  [per_device(): pl.pallas_call(kernel, out_shape=jax.ShapeDtypeStruct((GROUPS, 8, COLS),...]
where the time goes in v3:
time: 117 us; the launch traced here: 115 us
  Pallas kernels  113 us (97%)
  local copies, waits for them, and re-layouts  2.01 us (2%)
    pallas_call x1, Pallas kernels, per_device(): pl.pallas_call(kernel, out_shape=jax.ShapeDtypeStruct((GROUPS, 8, COLS),...  113 us

profile of v3, /device:TPU:0, one launch (start us, length us, event | category | flops | bytes accessed | tf_op | source)
XLA Modules:
  0.0 115.4 jit_solution(11617945791125075938)
XLA Ops:
  0.0 0.0 copy-start
  0.0 1.1 copy-done
  1.1 113.4 %shard_map.17 = f32[3,8,8192]{2,1,0:T(8,128)S(1)} custom-call(f32[3,8,8192]{2,1,0:T(8,128)S(1)} %bitcast.3), custom_call_target="tpu_custom_call" | custom-call | flops 10871635968 | bytes 1572864 | tf_op jit(solution)/shard_map/pallas_call | solution.py:390
  114.5 0.9 copy.3
Async XLA Ops:
  0.0 1.1 copy-start

commit v4 on v3

--- a/solution.py
+++ b/solution.py
@@ -318,7 +318,9 @@
             arrive(rise2[k - 5])
             arrive(fall2[k - 5])
         once(k)
-        if k > 1:
+        if k == 1:
+            pass_on(0)
+        if k > 2:
             pass_on(k - 2)
         if k > 3:
             far(k - 4)
@@ -349,7 +351,7 @@
     arrive(o_side["far"])
     for c in (5, 6, 7):
         twice(c)
-    T[...] = FACTOR * (3.4445 * X[mine] - 4.775 * O[mine] + 2.0315 * T[...])
+    T[...] = FACTOR * (2.0315 * T[...] - 4.775 * O[mine])
 
     before = list(leaving)
     i_out = fresh(o_ref.at[:, :, pl.ds(0, 15 * WIDTH)])
@@ -367,7 +369,7 @@
 
 
 def per_device(iterate):
-    vmem = pl.BlockSpec(memory_space=pltpu.VMEM)
+    anywhere = pl.BlockSpec(memory_space=pl.ANY)
     whole, gram, band = (BANDS, GROUPS, 4, 4, 8, WIDTH), (GROUPS, 4, 4, 8, ROWS), (BAND, ROWS)
     shapes = [
         (whole, F32),
@@ -387,11 +389,11 @@
         ((ROWS, WIDTH), BF16),
         ((GROUPS, 4, 4, 8, WIDTH), F32),
     ]
-    update = pl.pallas_call(
+    applied = pl.pallas_call(
         kernel,
         out_shape=jax.ShapeDtypeStruct((GROUPS, 8, COLS), F32),
-        in_specs=[vmem],
-        out_specs=vmem,
+        in_specs=[anywhere],
+        out_specs=anywhere,
         scratch_shapes=[pltpu.VMEM(shape, dtype) for shape, dtype in shapes]
         + [pltpu.SemaphoreType.DMA((N_SEMS,)), pltpu.SemaphoreType.DMA((N_SEMS,))],
         compiler_params=pltpu.CompilerParams(
@@ -401,7 +403,7 @@
             flops=6 * 3 * BAND * ROWS * WIDTH, bytes_accessed=2 * 4 * GROUPS * 8 * COLS, transcendentals=0
         ),
     )(iterate.reshape(GROUPS, 8, COLS))
-    return update.reshape(GROUPS * 8, COLS)
+    return FACTOR * 3.4445 * iterate + applied.reshape(GROUPS * 8, COLS)
 
 
 def solution(mesh):

time: 117 us -> 115 us (0.983); the launches traced: 115 us -> 115 us
  no operation moved by 1% of the time
where the time goes in v4:
time: 115 us
  Pallas kernels  113 us (98%)
    pallas_call x1, Pallas kernels, per_device(): pl.pallas_call(kernel, out_shape=jax.ShapeDtypeStruct((GROUPS, 8, COLS),...  113 us

profile of v4, /device:TPU:0, one launch (start us, length us, event | category | flops | bytes accessed | tf_op | source)
XLA Modules:
  0.0 114.8 jit_solution(4183928384112687325)
XLA Ops:
  0.0 0.0 copy-start
  0.0 1.1 copy-done
  1.1 112.7 %shard_map.17 = f32[3,8,8192]{2,1,0:T(8,128)S(1)} custom-call(f32[3,8,8192]{2,1,0:T(8,128)S(1)} %bitcast.3), custom_call_target="tpu_custom_call" | custom-call | flops 10871635968 | bytes 1572864 | tf_op jit(solution)/shard_map/pallas_call | solution.py:392
  113.8 1.0 bitcast_add_fusion
Async XLA Ops:
  0.0 1.1 copy-start

commit v5 on v4

--- a/solution.py
+++ b/solution.py
@@ -328,12 +328,15 @@
         at = slice(j * LANES, (j + 1) * LANES)
         Gh[at, :], Gl[at, :] = halves(G[j].reshape(LANES, ROWS))
 
+    def term(*chunk):
+        for c in chunk:
+            split(O, Oh, Ol, c)
+        at = slice(CHUNK[chunk[0]].start, CHUNK[chunk[-1]].stop)
+        gh, gl, oh, ol = Gh[:, at], Gl[:, at], Oh[at, :], Ol[at, :]
+        return (dot(gh, oh) + (dot(gl, oh) + dot(gh, ol))).reshape(GROUPS, 4, 4, 8, WIDTH)
+
     def twice(c):
-        split(O, Oh, Ol, c)
-        at = CHUNK[c]
-        gh, gl, oh, ol = Gh[:, at], Gl[:, at], Oh[at, :], Ol[at, :]
-        term = (dot(gh, oh) + (dot(gl, oh) + dot(gh, ol))).reshape(GROUPS, 4, 4, 8, WIDTH)
-        T[...] = T[...] + term if c else term
+        T[...] = T[...] + term(c) if c else term(c)
 
     twice(0)
     pass_on(5)
@@ -349,9 +352,7 @@
     far(5)
     far(6)
     arrive(o_side["far"])
-    for c in (5, 6, 7):
-        twice(c)
-    T[...] = FACTOR * (2.0315 * T[...] - 4.775 * O[mine])
+    T[...] = FACTOR * (2.0315 * (T[...] + term(5, 6, 7)) - 4.775 * O[mine])
 
     before = list(leaving)
     i_out = fresh(o_ref.at[:, :, pl.ds(0, 15 * WIDTH)])

time: 115 us -> 115 us (level)
  no operation moved by 1% of the time
where the time goes in v5:
time: 115 us
  Pallas kernels  113 us (98%)
    pallas_call x1, Pallas kernels, per_device(): pl.pallas_call(kernel, out_shape=jax.ShapeDtypeStruct((GROUPS, 8, COLS),...  113 us

profile of v5, /device:TPU:0, one launch (start us, length us, event | category | flops | bytes accessed | tf_op | source)
XLA Modules:
  0.0 114.8 jit_solution(11665811751854295407)
XLA Ops:
  0.0 0.0 copy-start
  0.0 1.1 copy-done
  1.1 112.7 %shard_map.17 = f32[3,8,8192]{2,1,0:T(8,128)S(1)} custom-call(f32[3,8,8192]{2,1,0:T(8,128)S(1)} %bitcast.3), custom_call_target="tpu_custom_call" | custom-call | flops 10871635968 | bytes 1572864 | tf_op jit(solution)/shard_map/pallas_call | solution.py:393
  113.8 1.0 bitcast_add_fusion
Async XLA Ops:
  0.0 1.1 copy-start
